TPU v7x, 128 devices: a whole 4x4x4 slice. The times are simulated.
128 devices in a mesh: grp: 4 (over x), fsdp: 32 (over y, z, core).
Axes of the slice: x: 4, y: 4, z: 4, core: 2. Of those that a mesh axis runs over, the one named last changes fastest.
Arguments:
- tokens: bfloat16 [8192, 4096], P('fsdp'), may hold values from -550 to 550
- attn_gain: float32 [4096], replicated, may hold values from 0.1 to 1.9
- ffn_gain: float32 [4096], replicated, may hold values from 0.1 to 1.9
- w_query: bfloat16 [4096, 4096], P('fsdp', 'grp'), may hold values from -2.421875 to 2.421875
- w_key: bfloat16 [4096, 256], P('fsdp'), may hold values from -0.078125 to 0.078125
- value_weight: bfloat16 [4096, 256], P('fsdp'), may hold values from -0.09375 to 0.09375
- w_out: bfloat16 [4096, 4096], P('grp', 'fsdp'), may hold values from -0.5 to 0.5
- routes: int32 [8192, 8], P('fsdp'), may hold values from 0 to 127, all different within a row; in each aligned block of 256 rows (0 to 255, 256 to 511, ...) at most 24 rows name the same one
- route_probs: bfloat16 [8192, 8], P('fsdp'), may hold values from 0.049804688 to 0.3984375
- w_gate_up: bfloat16 [128, 4096, 1536], P(('grp', 'fsdp')), may hold values from -0.09375 to 0.09375
- w_down: bfloat16 [128, 768, 4096], P(('grp', 'fsdp')), may hold values from -0.21875 to 0.21875
Outputs:
- attn_branch: bfloat16 [8192, 4096], P('fsdp')
- layer_out: bfloat16 [8192, 4096], P('fsdp', 'grp')
Inputs may be any that keep to these rules, and one draw needn't show every extreme that they name: `routes`: each row names 8 different experts. Among the 256 rows of one device (aligned blocks), no expert is named more than 24 times, a bound that some block reaches.
All inputs are finite; a program needn't handle non-finite values.
Results may differ from a plain program's by a relative error of at most 0.015.
Values may be sent and summed in bfloat16 or wider, within the bound.
No kernel may reach another device: no remote copies, remote signals or barrier semaphores. Data moves between devices by JAX's collectives and lax.ppermute only.
A program may use at most 128 MiB of HBM per device.

v0:
```python
import jax
import jax.numpy as jnp
from jax import lax
from jax.sharding import PartitionSpec as P

KEY_VALUE_HEADS = 2
HEAD_DIMENSION = 128
FFW = 768
EPSILON = 1e-06
FLOOR_SCORE = -1e30


def rms_scale(row_data, gain):
    floats = row_data.astype(jnp.float32)
    mean_sq = jnp.mean(floats * floats, axis=-1, keepdims=True)
    return (floats * lax.rsqrt(mean_sq + EPSILON) * gain).astype(jnp.bfloat16)


def attend_block(state, query_bf, key_block, value_block, key_start, positions):
    row_best, row_total, weighted = state
    scores = jnp.einsum(
        "thd,kd->thk", query_bf, key_block, preferred_element_type=jnp.float32
    ) * HEAD_DIMENSION ** (-0.5)
    key_pos = key_start + jnp.arange(key_block.shape[0], dtype=jnp.int32)
    allowed = (key_pos[None, :] <= positions[:, None])[:, None, :]
    masked = jnp.where(allowed, scores, FLOOR_SCORE)
    new_best = jnp.maximum(row_best, jnp.max(masked, axis=2))
    weights = jnp.where(allowed, jnp.exp(masked - new_best[:, :, None]), 0.0)
    rescale = jnp.exp(row_best - new_best)
    row_total = row_total * rescale + jnp.sum(weights, axis=2)
    weighted = weighted * rescale[:, :, None] + jnp.einsum(
        "thk,kd->thd", weights.astype(jnp.bfloat16), value_block, preferred_element_type=jnp.float32
    )
    return (new_best, row_total, weighted)


def on_device(
    tokens,
    attn_gain,
    ffn_gain,
    w_query,
    w_key,
    value_weight,
    w_out,
    routes,
    route_probs,
    w_gate_up,
    w_down,
):
    head_groups = lax.axis_size("grp")
    fsdp_size = lax.axis_size("fsdp")
    current_group = lax.axis_index("grp")
    my_rank = lax.axis_index("fsdp")
    tok_rows = tokens.shape[0]
    model_width = tokens.shape[1]
    head_width = w_query.shape[1]
    group_heads = head_width // HEAD_DIMENSION
    key_value_head = current_group * KEY_VALUE_HEADS // head_groups
    normed = rms_scale(tokens, attn_gain)
    key_cols = lax.dynamic_slice_in_dim(w_key, key_value_head * HEAD_DIMENSION, HEAD_DIMENSION, 1)
    value_cols = lax.dynamic_slice_in_dim(
        value_weight, key_value_head * HEAD_DIMENSION, HEAD_DIMENSION, 1
    )
    query = jnp.dot(
        normed,
        lax.all_gather(w_query, "fsdp", axis=0, tiled=True),
        preferred_element_type=jnp.float32,
    )
    key_local = jnp.dot(
        normed,
        lax.all_gather(key_cols, "fsdp", axis=0, tiled=True),
        preferred_element_type=jnp.float32,
    )
    value_local = jnp.dot(
        normed,
        lax.all_gather(value_cols, "fsdp", axis=0, tiled=True),
        preferred_element_type=jnp.float32,
    )
    query_bf = query.astype(jnp.bfloat16).reshape(tok_rows, group_heads, HEAD_DIMENSION)
    key_local = key_local.astype(jnp.bfloat16)
    value_local = value_local.astype(jnp.bfloat16)
    first_row = my_rank * tok_rows
    positions = first_row + jnp.arange(tok_rows, dtype=jnp.int32)
    last_query = first_row + tok_rows - 1
    attend_init = (
        jnp.full((tok_rows, group_heads), FLOOR_SCORE, jnp.float32),
        jnp.zeros((tok_rows, group_heads), jnp.float32),
        jnp.zeros((tok_rows, group_heads, HEAD_DIMENSION), jnp.float32),
    )
    state = attend_init
    key_rows = lax.all_gather(key_local, "fsdp", axis=0, tiled=True)
    value_rows = lax.all_gather(value_local, "fsdp", axis=0, tiled=True)
    row_count = key_rows.shape[0]
    key_span = 1024

    def visit(running, step_index):
        block_start = step_index * key_span
        key_block = lax.dynamic_slice_in_dim(key_rows, block_start, key_span, 0)
        value_block = lax.dynamic_slice_in_dim(value_rows, block_start, key_span, 0)
        needed = block_start <= last_query
        running = lax.cond(
            needed,
            lambda inner: attend_block(
                inner, query_bf, key_block, value_block, block_start, positions
            ),
            lambda inner: inner,
            running,
        )
        return (running, None)

    state, _ = lax.scan(visit, state, jnp.arange(row_count // key_span, dtype=jnp.int32))
    row_best, row_total, weighted = state
    attended = (weighted / row_total[:, :, None]).astype(jnp.bfloat16).reshape(tok_rows, head_width)
    head_part = jnp.dot(
        attended,
        lax.all_gather(w_out, "fsdp", axis=1, tiled=True),
        preferred_element_type=jnp.float32,
    ).astype(jnp.bfloat16)
    attn_branch = lax.psum(head_part.astype(jnp.float32).astype(jnp.bfloat16), "grp")
    resid = (tokens.astype(jnp.float32) + attn_branch.astype(jnp.float32)).astype(jnp.bfloat16)
    ffn_in = rms_scale(resid, ffn_gain)
    top_count = routes.shape[1]
    experts_all = head_groups * fsdp_size
    capacity = max(2, 3 * tok_rows * top_count // (2 * experts_all))
    group_rows = fsdp_size * capacity
    flat_routes = routes.reshape(-1)
    expert_hits = (
        flat_routes[:, None] == jnp.arange(experts_all, dtype=jnp.int32)[None, :]
    ).astype(jnp.int32)
    slot_ids = jnp.sum(jnp.cumsum(expert_hits, axis=0) * expert_hits, axis=1) - 1
    target = flat_routes * capacity + slot_ids
    local_target = target - current_group * group_rows
    slot_match = (
        local_target[:, None] == jnp.arange(group_rows, dtype=jnp.int32)[None, :]
    ).reshape(tok_rows, top_count, group_rows)
    chosen = jnp.any(slot_match, axis=1).astype(jnp.bfloat16)
    outbound = (
        jnp.einsum("tr,td->rd", chosen, ffn_in, preferred_element_type=jnp.float32)
        .astype(jnp.bfloat16)
        .reshape(fsdp_size, capacity, model_width)
    )
    gate_proj = w_gate_up[0]
    down_proj = w_down[0]
    col_width = model_width // head_groups
    arrived = lax.all_to_all(outbound, "fsdp", split_axis=0, concat_axis=0, tiled=True)
    slot_count = arrived.shape[1]
    arrived_rows = arrived.reshape(-1, model_width)
    gate_up = jnp.dot(arrived_rows, gate_proj, preferred_element_type=jnp.float32)
    hidden = (jax.nn.silu(gate_up[:, :FFW]) * gate_up[:, FFW:]).astype(jnp.bfloat16)
    result = jnp.dot(hidden, down_proj, preferred_element_type=jnp.float32).astype(jnp.bfloat16)
    returned = lax.all_to_all(
        result.reshape(fsdp_size, slot_count, model_width),
        "fsdp",
        split_axis=0,
        concat_axis=0,
        tiled=True,
    )
    mixing = jnp.sum(jnp.where(slot_match, route_probs[:, :, None], 0.0), axis=1)
    group_part = jnp.dot(
        mixing, returned.reshape(group_rows, model_width), preferred_element_type=jnp.float32
    ).astype(jnp.bfloat16)
    expert_mix = lax.psum_scatter(
        group_part.astype(jnp.float32).astype(jnp.bfloat16), "grp", scatter_dimension=1, tiled=True
    ).astype(jnp.float32)
    own_cols = lax.dynamic_slice_in_dim(resid, current_group * col_width, col_width, 1)
    layer_out = (own_cols.astype(jnp.float32) + expert_mix).astype(jnp.bfloat16)
    return (attn_branch, layer_out)


def solution(mesh):
    placed = (
        P("fsdp", None),
        P(),
        P(),
        P("fsdp", "grp"),
        P("fsdp", None),
        P("fsdp", None),
        P("grp", "fsdp"),
        P("fsdp", None),
        P("fsdp", None),
        P(("grp", "fsdp"), None, None),
        P(("grp", "fsdp"), None, None),
    )
    return jax.shard_map(
        on_device,
        mesh=mesh,
        in_specs=placed,
        out_specs=(P("fsdp", None), P("fsdp", "grp")),
        check_vma=False,
    )
```

profile of v0, /device:TPU:1, one launch (start us, length us, event | category | flops | bytes accessed | tf_op | source)
XLA Modules:
  0.0 637.4 jit_solution(16513742144885637357)
XLA Ops:
  7.3 0.7 copy-done
  8.0 0.6 constant_dynamic-slice_fusion
  8.7 0.0 all-gather.7.cloned.1.call-start
  8.7 1.4 constant_dynamic-slice_fusion.1
  10.1 0.0 all-gather.11.cloned.1.call-start
  10.2 0.7 all-gather.11.cloned.1.call-update
  10.9 2.1 fusion.29
  13.0 44.5 %all-gather.13.cloned.1.call-done = bf16[4096,128]{1,0:T(8,128)(2,1)} async-done(((bf16[128,128]{1,0:T(8,128)(2,1)}), bf16[4096,128]{1,0:T(8,128)(2,1)}) %all-gather.13.cloned.1.call-update) | async-done | bytes 1048592 | tf_op jit(solution)/shard_map/all_gather | solution.py:76
  57.5 3.3 convolution_convert_fusion.5
  60.8 0.0 all-gather.9.cloned.1.call-start
  60.9 41.6 %all-gather.7.cloned.1.call-done = bf16[4096,128]{1,0:T(8,128)(2,1)} async-done(((bf16[128,128]{1,0:T(8,128)(2,1)}), bf16[4096,128]{1,0:T(8,128)(2,1)}) %all-gather.7.cloned.1.call-update) | async-done | bytes 1048592 | tf_op jit(solution)/shard_map/all_gather | solution.py:71
  102.4 2.7 convolution_convert_fusion.6
  105.2 0.5 all-gather.17.cloned.1.call-update
  105.8 51.2 %all-gather.11.cloned.1.call-done = bf16[4096,1024]{1,0:T(8,128)(2,1)} async-done(((bf16[128,1024]{1,0:T(8,128)(2,1)}), bf16[4096,1024]{1,0:T(8,128)(2,1)}) %all-gather.11.cloned.1.call-update) | async-done | bytes 8388624 | tf_op jit(solution)/shard_map/all_gather | solution.py:66
  157.0 5.7 fusion.38
  162.7 0.1 copy.50
  162.8 40.4 %all-gather.15.cloned.1.call-done = bf16[8192,128]{1,0:T(8,128)(2,1)} async-done(((bf16[256,128]{1,0:T(8,128)(2,1)}), bf16[8192,128]{1,0:T(8,128)(2,1)}) %all-gather.15.cloned.1.call-update) | async-done | bytes 2097168 | tf_op jit(solution)/shard_map/all_gather | solution.py:92
  203.2 45.9 %all-gather.9.cloned.1.call-done = bf16[8192,128]{1,0:T(8,128)(2,1)} async-done(((bf16[256,128]{1,0:T(8,128)(2,1)}), bf16[8192,128]{1,0:T(8,128)(2,1)}) %all-gather.9.cloned.1.call-update) | async-done | bytes 2097168 | tf_op jit(solution)/shard_map/all_gather | solution.py:91
  249.1 0.1 broadcast_in_dim.65
  249.2 19.2 %while.15 = (s32[]{:T(128)}, f32[256,8]{0,1:T(8,128)S(1)}, f32[256,8]{0,1:T(8,128)S(1)}, f32[256,8,128]{2,0,1:T(8,128)S(1)}, s32[8]{0:T(128)S(1)}, /*index=5*/s3...) while((s32[]{:T(128)}, f32[256,8]{0,1:T(8,128)S(1)}, ...), condition=%wide.region_6.7_spmd.clone, body=%wide.region_1.6_spmd.clone.sunk | while | flops 1101796608 | bytes 29503820 | solution.py:111
  249.4 0.6 dynamic_slice.49
  250.7 8.7 %conditional.3 = ((f32[256,8]{0,1:T(8,128)S(1)}, f32[256,8]{0,1:T(8,128)S(1)}, f32[256,8,128]{2,0,1:T(8,128)S(1)})) conditional(s32[]{:T(128)} %convert_element_type.154, (f32[256,8]{0,1:T(8,128)S(1)}, f32[256,8]{0,1:T(8,128)S(1)}, f32[256,8,128]{2,0,1:T(8,128)S(1)}) %tuple.52, (s32[]{:T(128)}, s32[]{:T(128)}, bf16[8192,128]{1,0:T(8,128)(2,1)}, ...), branch_computations={%region_2.2_spmd, %region_3.5_spmd} | conditional | flops 1101796608 | bytes 29502546 | solution.py:101
  250.7 0.2 broadcast_compare_fusion
  250.9 2.4 fusion.2
  253.3 2.0 fusion.4
  255.4 3.9 fusion.8
  259.4 0.6 dynamic_slice.49
  260.7 0.6 dynamic_slice.49
  262.0 0.6 dynamic_slice.49
  263.3 0.6 dynamic_slice.49
  264.6 0.6 dynamic_slice.49
  265.8 0.6 dynamic_slice.49
  267.1 0.6 dynamic_slice.49
  268.4 0.3 copy.39
  268.8 0.1 divide_convert_fusion
  268.9 41.3 %all-gather.17.cloned.1.call-done = bf16[1024,4096]{1,0:T(8,128)(2,1)} async-done(((bf16[1024,128]{1,0:T(8,128)(2,1)}), bf16[1024,4096]{1,0:T(8,128)(2,1)}) %all-gather.17.cloned.1.call-update) | async-done | bytes 8388624 | tf_op jit(solution)/shard_map/all_gather | solution.py:116
  310.1 7.1 %convolution_convert_fusion.2 = bf16[256,4096]{1,0:T(8,128)(2,1)} fusion(bf16[256,1024]{0,1:T(8,128)(2,1)S(1)} %bitcast.62, bf16[1024,4096]{1,0:T(8,128)(2,1)} %all-gather.17.cloned.1.call-done), kind=kOutput, calls=%fused_computation.37 | convolution fusion | flops 2148532224 | bytes 11010048 | tf_op jit(solution)/shard_map/dot_general | solution.py:114
  317.2 0.1 copy.40
  317.4 0.1 eq.43
  317.5 0.1 eq.39
  317.6 0.1 copy.42
  317.7 0.3 fusion.42
  318.1 0.1 broadcast_add_fusion.1
  318.2 0.3 copy.43
  318.5 0.6 fusion.41
  319.2 0.1 sub.46
  319.3 0.1 copy.44
  319.4 0.1 copy.45
  319.5 2.3 fusion.24
  321.8 72.3 %all-reduce.2.cloned.1.call-done = bf16[256,4096]{1,0:T(8,128)(2,1)} async-done(((bf16[256,4096]{1,0:T(8,128)(2,1)}), bf16[256,4096]{1,0:T(8,128)(2,1)}) %all-reduce.2.cloned.1.call-update) | async-done | bytes 2097168 | tf_op jit(solution)/shard_map/psum | solution.py:119
  394.1 3.2 fusion.26
  397.4 2.0 convolution_convert_fusion
  399.3 80.9 %all_to_all.10 = bf16[32,24,4096]{2,1,0:T(8,128)(2,1)S(1)} all-to-all(bf16[32,24,4096]{2,1,0:T(8,128)(2,1)S(1)} %bitcast.58), channel_id=1, replica_groups=mesh['grp'=4,'fsdp'=32] {'fsdp'}, dimensions={0} | all-to-all | bytes 12582912 | tf_op jit(solution)/shard_map/all_to_all | solution.py:145
  480.2 11.7 %fusion.21 = f32[768,1536]{1,0:T(8,128)} fusion(bf16[768,4096]{1,0:T(8,128)(2,1)S(1)} %bitcast.61, bf16[1,4096,1536]{2,1,0:T(8,128)(2,1)S(1)} %bitcast.64), kind=kOutput, calls=%fused_computation.24 | convolution fusion | flops 9663676416 | bytes 23592960 | tf_op jit(solution)/shard_map/dot_general | solution.py:148
  491.9 10.3 %convolution_convert_fusion.1 = bf16[768,4096]{1,0:T(8,128)(2,1)} fusion(bf16[1,768,4096]{2,1,0:T(8,128)(2,1)} %param.25, f32[768,1536]{1,0:T(8,128)} %fusion.21), kind=kOutput, calls=%fused_computation.27 | convolution fusion | flops 4838522880 | bytes 17301504 | tf_op jit(solution)/shard_map/dot_general | solution.py:150
  502.2 4.8 all-to-all-start.1
  507.0 0.0 reduce-scatter.2.cloned.1.call-start
  507.1 0.1 copy.46
  507.2 2.4 fusion.33
  509.6 75.3 %all-to-all-done.1 = bf16[32,24,4096]{2,1,0:T(8,128)(2,1)} async-done(((bf16[32,24,4096]{2,1,0:T(8,128)(2,1)}), bf16[32,24,4096]{2,1,0:T(8,128)(2,1)}, u32[]{:S(2)}, u32[]{:S(2)}) %all-to-all-start.1) | async-done | bytes 6291488 | tf_op jit(solution)/shard_map/all_to_all | solution.py:151
  584.8 5.9 convolution_convert_fusion.3
  590.8 34.6 %reduce-scatter.2.cloned.1.call-done = bf16[256,1024]{1,0:T(8,128)(2,1)} async-done(((bf16[256,4096]{1,0:T(8,128)(2,1)}), bf16[256,1024]{1,0:T(8,128)(2,1)}) %reduce-scatter.2.cloned.1.call-update) | async-done | bytes 524304 | tf_op jit(solution)/shard_map/reduce_scatter | solution.py:162
  625.4 2.0 add_convert_fusion
  627.4 3.1 copy.70
  (60 shorter events, 0.5 us)
Async XLA Ops:
  7.2 0.8 copy-start
  7.2 95.3 %copy-start.2 = (bf16[256,4096]{1,0:T(8,128)(2,1)S(1)}, bf16[256,4096]{1,0:T(8,128)(2,1)}, u32[]{:S(2)}) copy-start(bf16[256,4096]{1,0:T(8,128)(2,1)} %param.15) | copy-start | bytes 6291460
  7.2 95.3 %copy-start.6 = (f32[4096]{0:T(1024)S(1)}, f32[4096]{0:T(1024)}, u32[]{:S(2)}) copy-start(f32[4096]{0:T(1024)} %param.16) | copy-start | bytes 49156
  7.2 50.3 %all-gather.13.cloned.1.call-start = ((), (), s32[]{:S(2)}) async-start(), calls=%async_computation.6 | async-start | bytes 1081344 | tf_op jit(solution)/shard_map/all_gather | solution.py:76
  8.7 93.8 %all-gather.7.cloned.1.call-start = ((), (), s32[]{:S(2)}) async-start(), calls=%async_computation.3 | async-start | bytes 1081344 | tf_op jit(solution)/shard_map/all_gather | solution.py:71
  10.1 146.8 %all-gather.11.cloned.1.call-start = ((), (), s32[]{:S(2)}) async-start(), calls=%async_computation.5 | async-start | bytes 8650752 | tf_op jit(solution)/shard_map/all_gather | solution.py:66
  10.8 192.3 %all-gather.15.cloned.1.call-start = ((), (), s32[]{:S(2)}) async-start(), calls=%async_computation.7 | async-start | bytes 2162688 | tf_op jit(solution)/shard_map/all_gather | solution.py:92
  60.8 188.3 %all-gather.9.cloned.1.call-start = ((), (), s32[]{:S(2)}) async-start(), calls=%async_computation.4 | async-start | bytes 2162688 | tf_op jit(solution)/shard_map/all_gather | solution.py:91
  105.1 205.0 %all-gather.17.cloned.1.call-start = ((), (), s32[]{:S(2)}) async-start(), calls=%async_computation.8 | async-start | bytes 8650752 | tf_op jit(solution)/shard_map/all_gather | solution.py:116
  105.7 288.4 %all-reduce.2.cloned.1.call-start = ((), (), s32[]{:S(2)}) async-start(), calls=%async_computation.9 | async-start | bytes 4194304 | tf_op jit(solution)/shard_map/psum | solution.py:119
  310.1 7.1 %copy-start.3 = (s32[256,8]{0,1:T(8,128)S(1)}, s32[256,8]{0,1:T(8,128)}, u32[]{:S(2)}) copy-start(s32[256,8]{0,1:T(8,128)} %param.22) | copy-start | bytes 24580
  318.5 78.8 %copy-start.4 = (f32[4096]{0:T(1024)S(1)}, f32[4096]{0:T(1024)}, u32[]{:S(2)}) copy-start(f32[4096]{0:T(1024)} %param.17) | copy-start | bytes 49156
  397.3 82.9 %slice-start = ((s8[12582912]{0:T(1024)(128)(4,1)}), s8[4194304]{0:T(1024)(128)(4,1)S(1)}, s32[]{:S(2)}) async-start(s8[12582912]{0:T(1024)(128)(4,1)} %bitcast.63), calls=%async_computation.11 | async-start | bytes 8388608
  397.3 82.9 %slice-start.1 = ((s8[12582912]{0:T(1024)(128)(4,1)}), s8[4194304]{0:T(1024)(128)(4,1)S(1)}, s32[]{:S(2)}) async-start(s8[12582912]{0:T(1024)(128)(4,1)} %bitcast.63), calls=%async_computation.12 | async-start | bytes 8388608
  399.3 80.9 %slice-start.2 = ((s8[12582912]{0:T(1024)(128)(4,1)}), s8[4194304]{0:T(1024)(128)(4,1)S(1)}, s32[]{:S(2)}) async-start(s8[12582912]{0:T(1024)(128)(4,1)} %bitcast.63), calls=%async_computation.13 | async-start | bytes 8388608
  502.2 4.9 copy-start.5
  502.2 82.7 %all-to-all-start.1 = ((bf16[32,24,4096]{2,1,0:T(8,128)(2,1)}), bf16[32,24,4096]{2,1,0:T(8,128)(2,1)}, u32[]{:S(2)}, u32[]{:S(2)}) async-start(bf16[32,24,4096]{2,1,0:T(8,128)(2,1)} %bitcast.60), calls=%async_computation.1 | async-start | bytes 12582912 | tf_op jit(solution)/shard_map/all_to_all | solution.py:151
  507.0 118.4 %reduce-scatter.2.cloned.1.call-start = ((), (), s32[]{:S(2)}) async-start(), calls=%async_computation.10 | async-start | bytes 2621440 | tf_op jit(solution)/shard_map/reduce_scatter | solution.py:162
  584.8 45.7 %copy-start.1 = (bf16[128,256]{1,0:T(8,128)(2,1)S(1)}, bf16[128,256]{1,0:T(8,128)(2,1)}, u32[]{:S(2)}) copy-start(bf16[128,256]{1,0:T(8,128)(2,1)} %param.20) | copy-start | bytes 196612
Sparse Core Ops, SparseCore 0:
  10.9 46.5 all-gather.12
  60.3 42.0 all-gather.6
  104.7 52.1 all-gather.10
  159.6 43.4 all-gather.14
  205.9 43.2 all-gather.8
  251.2 58.9 all-gather.16
  317.4 76.7 all-reduce.1
  590.9 34.4 reduce-scatter.1
where the time goes:
time: 638 us; the launch traced here: 637 us
  waiting for transfers between devices  448 us (70%)
  blocking collectives  80.9 us (13%)
  matrix products  55 us (9%)
  other arithmetic  15.4 us (2%)
  between operations  14.4 us (2%)
  local copies, waits for them, and re-layouts  12.3 us (2%)
    all_to_all x1, blocking collectives, on_device(): lax.all_to_all(outbound, 'fsdp', split_axis=0, concat_axis=0, tiled=True)  80.9 us
    all_to_all x1, waiting for transfers between devices, on_device(): lax.all_to_all(result.reshape(fsdp_size, slot_count, model_width), 'fsdp'...  75.3 us
    psum x1, waiting for transfers between devices, on_device(): lax.psum(head_part.astype(jnp.float32).astype(jnp.bfloat16), 'grp')  72.3 us
    all_gather x1, waiting for transfers between devices, on_device(): lax.all_gather(w_query, 'fsdp', axis=0, tiled=True)  51.2 us
    all_gather x1, waiting for transfers between devices, on_device(): key_rows = lax.all_gather(key_local, 'fsdp', axis=0, tiled=True)  45.9 us
    all_gather x1, waiting for transfers between devices, on_device(): lax.all_gather(value_cols, 'fsdp', axis=0, tiled=True)  44.5 us
    all_gather x1, waiting for transfers between devices, on_device(): lax.all_gather(key_cols, 'fsdp', axis=0, tiled=True)  41.6 us
    all_gather x1, waiting for transfers between devices, on_device(): lax.all_gather(w_out, 'fsdp', axis=1, tiled=True)  41.3 us
  transfers between devices with their start and end apart: 9, of which 9 were waited for; matrix products, arithmetic and copies ran while one was open for 6% of the time, Pallas kernels for 0%

commit v1 on v0

--- a/solution.py
+++ b/solution.py
@@ -113,7 +113,9 @@
     attended = (weighted / row_total[:, :, None]).astype(jnp.bfloat16).reshape(tok_rows, head_width)
     head_part = jnp.dot(
         attended,
-        lax.all_gather(w_out, "fsdp", axis=1, tiled=True),
+        jnp.concatenate(
+            lax.all_to_all(jnp.stack([w_out] * lax.axis_size("fsdp")), "fsdp", 0, 0), axis=1
+        ),
         preferred_element_type=jnp.float32,
     ).astype(jnp.bfloat16)
     attn_branch = lax.psum(head_part.astype(jnp.float32).astype(jnp.bfloat16), "grp")

time: 638 us -> 710 us (1.11)
  waiting for transfers between devices: 448 us -> 510 us
    all_gather x1, waiting for transfers between devices: 41.6 us -> 97.3 us  [on_device(): lax.all_gather(key_cols, 'fsdp', axis=0, tiled=True)]
    all_gather x1 -> x0, waiting for transfers between devices: 41.3 us -> none  [on_device(): lax.all_gather(w_out, 'fsdp', axis=1, tiled=True)]
    psum x1, waiting for transfers between devices: 72.3 us -> 113 us  [on_device(): lax.psum(head_part.astype(jnp.float32).astype(jnp.bfloat16), 'grp')]
  transfers between devices with their start and end apart: 9 -> 9, of which waited for: 9 -> 8; matrix products, arithmetic and copies ran while one was open for 6% -> 6% of each run, Pallas kernels for 0% -> 0%
where the time goes in v1:
time: 710 us; the launch traced here: 709 us
  waiting for transfers between devices  510 us (72%)
  blocking collectives  80.9 us (11%)
  matrix products  55.1 us (8%)
  local copies, waits for them, and re-layouts  16.8 us (2%)
  other arithmetic  15.4 us (2%)
  between operations  14.5 us (2%)
  starting transfers between devices  10.5 us (1%)
    psum x1, waiting for transfers between devices, on_device(): lax.psum(head_part.astype(jnp.float32).astype(jnp.bfloat16), 'grp')  113 us
    all_gather x1, waiting for transfers between devices, on_device(): lax.all_gather(key_cols, 'fsdp', axis=0, tiled=True)  97.3 us
    all_to_all x1, blocking collectives, on_device(): lax.all_to_all(outbound, 'fsdp', split_axis=0, concat_axis=0, tiled=True)  80.9 us
    all_to_all x1, waiting for transfers between devices, on_device(): lax.all_to_all(result.reshape(fsdp_size, slot_count, model_width), 'fsdp'...  75.3 us
    all_gather x1, waiting for transfers between devices, on_device(): lax.all_gather(w_query, 'fsdp', axis=0, tiled=True)  57.6 us
    all_gather x1, waiting for transfers between devices, on_device(): key_rows = lax.all_gather(key_local, 'fsdp', axis=0, tiled=True)  45.9 us
    all_gather x1, waiting for transfers between devices, on_device(): lax.all_gather(value_cols, 'fsdp', axis=0, tiled=True)  44.5 us
    all_gather x1, waiting for transfers between devices, on_device(): value_rows = lax.all_gather(value_local, 'fsdp', axis=0, tiled=True)  40.3 us
  transfers between devices with their start and end apart: 9, of which 8 were waited for; matrix products, arithmetic and copies ran while one was open for 6% of the time, Pallas kernels for 0%

profile of v1, /device:TPU:1, one launch (start us, length us, event | category | flops | bytes accessed | tf_op | source)
XLA Modules:
  0.0 708.6 jit_solution(4817414455475620107)
XLA Ops:
  7.3 0.8 copy-done
  8.0 0.6 constant_dynamic-slice_fusion
  8.7 0.0 all-gather.6.cloned.1.call-start
  8.7 1.4 constant_dynamic-slice_fusion.1
  10.2 0.7 all-gather.10.cloned.1.call-update
  10.9 2.1 fusion.29
  13.0 44.5 %all-gather.12.cloned.1.call-done = bf16[4096,128]{1,0:T(8,128)(2,1)} async-done(((bf16[128,128]{1,0:T(8,128)(2,1)}), bf16[4096,128]{1,0:T(8,128)(2,1)}) %all-gather.12.cloned.1.call-update) | async-done | bytes 1048592 | tf_op jit(solution)/shard_map/all_gather | solution.py:76
  57.5 3.3 convolution_convert_fusion.5
  60.8 0.1 copy.42
  61.0 4.3 stack.2
  65.3 5.4 all-to-all-start
  70.6 0.0 all-gather.8.cloned.1.call-start
  70.7 97.3 %all-gather.6.cloned.1.call-done = bf16[4096,128]{1,0:T(8,128)(2,1)} async-done(((bf16[128,128]{1,0:T(8,128)(2,1)}), bf16[4096,128]{1,0:T(8,128)(2,1)}) %all-gather.6.cloned.1.call-update) | async-done | bytes 1048592 | tf_op jit(solution)/shard_map/all_gather | solution.py:71
  168.0 2.7 convolution_convert_fusion.6
  170.7 0.0 all-reduce.2.cloned.1.call-start
  170.7 57.6 %all-gather.10.cloned.1.call-done = bf16[4096,1024]{1,0:T(8,128)(2,1)} async-done(((bf16[128,1024]{1,0:T(8,128)(2,1)}), bf16[4096,1024]{1,0:T(8,128)(2,1)}) %all-gather.10.cloned.1.call-update) | async-done | bytes 8388624 | tf_op jit(solution)/shard_map/all_gather | solution.py:66
  228.3 5.8 fusion.38
  234.0 0.1 copy.53
  234.1 40.3 %all-gather.14.cloned.1.call-done = bf16[8192,128]{1,0:T(8,128)(2,1)} async-done(((bf16[256,128]{1,0:T(8,128)(2,1)}), bf16[8192,128]{1,0:T(8,128)(2,1)}) %all-gather.14.cloned.1.call-update) | async-done | bytes 2097168 | tf_op jit(solution)/shard_map/all_gather | solution.py:92
  274.5 45.9 %all-gather.8.cloned.1.call-done = bf16[8192,128]{1,0:T(8,128)(2,1)} async-done(((bf16[256,128]{1,0:T(8,128)(2,1)}), bf16[8192,128]{1,0:T(8,128)(2,1)}) %all-gather.8.cloned.1.call-update) | async-done | bytes 2097168 | tf_op jit(solution)/shard_map/all_gather | solution.py:91
  320.4 0.1 broadcast_in_dim.65
  320.5 19.2 %while.15 = (s32[]{:T(128)}, f32[256,8]{0,1:T(8,128)S(1)}, f32[256,8]{0,1:T(8,128)S(1)}, f32[256,8,128]{2,0,1:T(8,128)S(1)}, s32[8]{0:T(128)S(1)}, /*index=5*/s3...) while((s32[]{:T(128)}, f32[256,8]{0,1:T(8,128)S(1)}, ...), condition=%wide.region_6.7_spmd.clone, body=%wide.region_1.6_spmd.clone.sunk | while | flops 1101796608 | bytes 29503820 | solution.py:111
  320.7 0.6 dynamic_slice.49
  322.0 8.7 %conditional.3 = ((f32[256,8]{0,1:T(8,128)S(1)}, f32[256,8]{0,1:T(8,128)S(1)}, f32[256,8,128]{2,0,1:T(8,128)S(1)})) conditional(s32[]{:T(128)} %convert_element_type.154, (f32[256,8]{0,1:T(8,128)S(1)}, f32[256,8]{0,1:T(8,128)S(1)}, f32[256,8,128]{2,0,1:T(8,128)S(1)}) %tuple.52, (s32[]{:T(128)}, s32[]{:T(128)}, bf16[8192,128]{1,0:T(8,128)(2,1)}, ...), branch_computations={%region_2.2_spmd, %region_3.5_spmd} | conditional | flops 1101796608 | bytes 29502546 | solution.py:101
  322.0 0.2 broadcast_compare_fusion
  322.2 2.4 fusion.2
  324.7 2.0 fusion.4
  326.7 3.9 fusion.8
  330.7 0.6 dynamic_slice.49
  332.0 0.6 dynamic_slice.49
  333.3 0.6 dynamic_slice.49
  334.6 0.6 dynamic_slice.49
  335.9 0.6 dynamic_slice.49
  337.1 0.6 dynamic_slice.49
  338.4 0.6 dynamic_slice.49
  339.7 0.3 copy.41
  340.1 0.1 divide_convert_fusion
  340.2 7.1 %convolution_convert_fusion.2 = bf16[256,4096]{1,0:T(8,128)(2,1)} fusion(bf16[256,1024]{0,1:T(8,128)(2,1)S(1)} %bitcast.65, bf16[1024,4096]{0,1:T(8,128)(2,1)} %bitcast.5), kind=kOutput, calls=%fused_computation.37 | convolution fusion | flops 2148532224 | bytes 11010048 | tf_op jit(solution)/shard_map/dot_general | solution.py:114
  347.3 0.1 copy.43
  347.5 0.1 eq.43
  347.6 0.1 eq.39
  347.7 0.1 copy.45
  347.8 0.3 fusion.42
  348.2 0.1 broadcast_add_fusion.1
  348.3 0.3 copy.46
  348.6 0.6 fusion.41
  349.3 0.1 sub.46
  349.4 0.1 copy.47
  349.4 0.1 copy.48
  349.6 2.3 fusion.24
  351.9 113.5 %all-reduce.2.cloned.1.call-done = bf16[256,4096]{1,0:T(8,128)(2,1)} async-done(((bf16[256,4096]{1,0:T(8,128)(2,1)}), bf16[256,4096]{1,0:T(8,128)(2,1)}) %all-reduce.2.cloned.1.call-update) | async-done | bytes 2097168 | tf_op jit(solution)/shard_map/psum | solution.py:121
  465.4 3.2 fusion.26
  468.6 2.0 convolution_convert_fusion
  470.6 80.9 %all_to_all.15 = bf16[32,24,4096]{2,1,0:T(8,128)(2,1)S(1)} all-to-all(bf16[32,24,4096]{2,1,0:T(8,128)(2,1)S(1)} %bitcast.61), channel_id=1, replica_groups=mesh['grp'=4,'fsdp'=32] {'fsdp'}, dimensions={0} | all-to-all | bytes 12582912 | tf_op jit(solution)/shard_map/all_to_all | solution.py:147
  551.4 11.7 %fusion.21 = f32[768,1536]{1,0:T(8,128)} fusion(bf16[768,4096]{1,0:T(8,128)(2,1)S(1)} %bitcast.64, bf16[1,4096,1536]{2,1,0:T(8,128)(2,1)S(1)} %bitcast.67), kind=kOutput, calls=%fused_computation.24 | convolution fusion | flops 9663676416 | bytes 23592960 | tf_op jit(solution)/shard_map/dot_general | solution.py:150
  563.1 10.3 %convolution_convert_fusion.1 = bf16[768,4096]{1,0:T(8,128)(2,1)} fusion(bf16[1,768,4096]{2,1,0:T(8,128)(2,1)} %param.25, f32[768,1536]{1,0:T(8,128)} %fusion.21), kind=kOutput, calls=%fused_computation.27 | convolution fusion | flops 4838522880 | bytes 17301504 | tf_op jit(solution)/shard_map/dot_general | solution.py:152
  573.4 4.8 all-to-all-start.2
  578.3 0.1 copy.49
  578.4 2.4 fusion.33
  580.8 75.3 %all-to-all-done.2 = bf16[32,24,4096]{2,1,0:T(8,128)(2,1)} async-done(((bf16[32,24,4096]{2,1,0:T(8,128)(2,1)}), bf16[32,24,4096]{2,1,0:T(8,128)(2,1)}, u32[]{:S(2)}, u32[]{:S(2)}) %all-to-all-start.2) | async-done | bytes 6291488 | tf_op jit(solution)/shard_map/all_to_all | solution.py:153
  656.1 5.9 convolution_convert_fusion.3
  662.0 34.6 %reduce-scatter.2.cloned.1.call-done = bf16[256,1024]{1,0:T(8,128)(2,1)} async-done(((bf16[256,4096]{1,0:T(8,128)(2,1)}), bf16[256,1024]{1,0:T(8,128)(2,1)}) %reduce-scatter.2.cloned.1.call-update) | async-done | bytes 524304 | tf_op jit(solution)/shard_map/reduce_scatter | solution.py:164
  696.6 2.0 add_convert_fusion
  698.7 3.1 copy.73
  (63 shorter events, 0.5 us)
Async XLA Ops:
  7.2 0.8 copy-start
  7.2 53.6 %copy-start.3 = (bf16[1024,128]{1,0:T(8,128)(2,1)S(1)}, bf16[1024,128]{1,0:T(8,128)(2,1)}, u32[]{:S(2)}) copy-start(bf16[1024,128]{1,0:T(8,128)(2,1)} %param.21) | copy-start | bytes 786436
  7.2 50.3 %all-gather.12.cloned.1.call-start = ((), (), s32[]{:S(2)}) async-start(), calls=%async_computation.7 | async-start | bytes 1081344 | tf_op jit(solution)/shard_map/all_gather | solution.py:76
  8.7 159.3 %all-gather.6.cloned.1.call-start = ((), (), s32[]{:S(2)}) async-start(), calls=%async_computation.4 | async-start | bytes 1081344 | tf_op jit(solution)/shard_map/all_gather | solution.py:71
  10.1 218.2 %all-gather.10.cloned.1.call-start = ((), (), s32[]{:S(2)}) async-start(), calls=%async_computation.6 | async-start | bytes 8650752 | tf_op jit(solution)/shard_map/all_gather | solution.py:66
  10.8 263.6 %all-gather.14.cloned.1.call-start = ((), (), s32[]{:S(2)}) async-start(), calls=%async_computation.8 | async-start | bytes 2162688 | tf_op jit(solution)/shard_map/all_gather | solution.py:92
  65.3 102.7 %copy-start.2 = (bf16[256,4096]{1,0:T(8,128)(2,1)S(1)}, bf16[256,4096]{1,0:T(8,128)(2,1)}, u32[]{:S(2)}) copy-start(bf16[256,4096]{1,0:T(8,128)(2,1)} %param.15) | copy-start | bytes 6291460
  65.3 102.7 %copy-start.7 = (f32[4096]{0:T(1024)S(1)}, f32[4096]{0:T(1024)}, u32[]{:S(2)}) copy-start(f32[4096]{0:T(1024)} %param.16) | copy-start | bytes 49156
  65.3 274.9 %all-to-all-start = ((bf16[32,1024,128]{1,2,0:T(8,128)(2,1)}), bf16[32,1024,128]{1,2,0:T(8,128)(2,1)}, u32[]{:S(2)}, u32[]{:S(2)}) async-start(bf16[32,1024,128]{1,2,0:T(8,128)(2,1)} %stack.2), calls=%async_computation | async-start | bytes 16777216 | tf_op jit(solution)/shard_map/all_to_all | solution.py:117
  70.6 249.8 %all-gather.8.cloned.1.call-start = ((), (), s32[]{:S(2)}) async-start(), calls=%async_computation.5 | async-start | bytes 2162688 | tf_op jit(solution)/shard_map/all_gather | solution.py:91
  170.7 294.7 %all-reduce.2.cloned.1.call-start = ((), (), s32[]{:S(2)}) async-start(), calls=%async_computation.9 | async-start | bytes 4194304 | tf_op jit(solution)/shard_map/psum | solution.py:121
  340.2 7.1 %copy-start.4 = (s32[256,8]{0,1:T(8,128)S(1)}, s32[256,8]{0,1:T(8,128)}, u32[]{:S(2)}) copy-start(s32[256,8]{0,1:T(8,128)} %param.22) | copy-start | bytes 24580
  348.6 119.9 %copy-start.5 = (f32[4096]{0:T(1024)S(1)}, f32[4096]{0:T(1024)}, u32[]{:S(2)}) copy-start(f32[4096]{0:T(1024)} %param.17) | copy-start | bytes 49156
  468.6 82.9 %slice-start = ((s8[12582912]{0:T(1024)(128)(4,1)}), s8[4194304]{0:T(1024)(128)(4,1)S(1)}, s32[]{:S(2)}) async-start(s8[12582912]{0:T(1024)(128)(4,1)} %bitcast.66), calls=%async_computation.11 | async-start | bytes 8388608
  468.6 82.9 %slice-start.1 = ((s8[12582912]{0:T(1024)(128)(4,1)}), s8[4194304]{0:T(1024)(128)(4,1)S(1)}, s32[]{:S(2)}) async-start(s8[12582912]{0:T(1024)(128)(4,1)} %bitcast.66), calls=%async_computation.12 | async-start | bytes 8388608
  470.5 80.9 %slice-start.2 = ((s8[12582912]{0:T(1024)(128)(4,1)}), s8[4194304]{0:T(1024)(128)(4,1)S(1)}, s32[]{:S(2)}) async-start(s8[12582912]{0:T(1024)(128)(4,1)} %bitcast.66), calls=%async_computation.13 | async-start | bytes 8388608
  573.4 4.9 copy-start.6
  573.4 82.7 %all-to-all-start.2 = ((bf16[32,24,4096]{2,1,0:T(8,128)(2,1)}), bf16[32,24,4096]{2,1,0:T(8,128)(2,1)}, u32[]{:S(2)}, u32[]{:S(2)}) async-start(bf16[32,24,4096]{2,1,0:T(8,128)(2,1)} %bitcast.63), calls=%async_computation.2 | async-start | bytes 12582912 | tf_op jit(solution)/shard_map/all_to_all | solution.py:153
  578.2 118.4 %reduce-scatter.2.cloned.1.call-start = ((), (), s32[]{:S(2)}) async-start(), calls=%async_computation.10 | async-start | bytes 2621440 | tf_op jit(solution)/shard_map/reduce_scatter | solution.py:164
  656.1 45.7 %copy-start.1 = (bf16[128,256]{1,0:T(8,128)(2,1)S(1)}, bf16[128,256]{1,0:T(8,128)(2,1)}, u32[]{:S(2)}) copy-start(bf16[128,256]{1,0:T(8,128)(2,1)} %param.20) | copy-start | bytes 196612
Sparse Core Ops, SparseCore 0:
  10.9 46.5 all-gather.11
  60.3 107.6 all-gather.5
  170.2 58.0 all-gather.9
  231.0 43.4 all-gather.13
  277.2 43.2 all-gather.7
  347.4 117.8 all-reduce.1
  662.2 34.4 reduce-scatter.1
